TPU v7x, 32 devices: a whole 2x2x4 slice. The times are simulated.
32 devices in a mesh: grp: 4 (over z), aux: 8 (over y, x, core).
Axes of the slice: x: 2, y: 2, z: 4, core: 2. Of those that a mesh axis runs over, the one named last changes fastest.
Arguments:
- integrals: bfloat16 [1536, 512, 512], P('aux', 'grp'), may hold values from -0.01953125 to 0.01953125
- coefficients: bfloat16 [96, 8, 64], replicated, may hold values from -0.375 to 0.375
- block_lists: int32 [96, 8], replicated, may hold values from 0 to 7, as said below
- block_counts: int32 [96], replicated, may hold values from 1 to 8
Outputs:
- exchange_matrix: float32 [512, 512], P(('grp', 'aux'))
Inputs may be any that keep to these rules, and one draw needn't show every extreme that they name: `block_lists`: the entries of one row are distinct blocks.
All inputs are finite; a program needn't handle non-finite values.
Results may differ from a plain program's by a relative error of at most 0.00031.
Values may be sent and summed in bfloat16 or wider, within the bound.
A program may use at most 128 MiB of HBM per device.

v0:
```python
import jax
import jax.numpy as jnp
from jax import lax
from jax.sharding import PartitionSpec as P


def block_tables(block_rows, counts, block_total):
    slot = lax.broadcasted_iota(jnp.int32, block_rows.shape, 1)
    live_slot = slot < counts[:, None]
    target = lax.broadcasted_iota(jnp.int32, block_rows.shape + (block_total,), 2)
    onehot = (block_rows[:, :, None] == target) & live_slot[:, :, None]
    return onehot.astype(jnp.bfloat16)


def shards(integrals, coefficients, block_lists, block_counts):
    window = integrals.shape[2]
    block_size = coefficients.shape[2]
    block_total = window // block_size
    orbitals = coefficients.shape[0]
    selected = block_tables(block_lists, block_counts, block_total)
    columns = jnp.einsum("ikb,ikj->bji", selected, coefficients, preferred_element_type=jnp.float32)
    columns = columns.astype(jnp.bfloat16).reshape(window, orbitals)
    half_rows = jnp.einsum(
        "pmn,ni->pim", integrals, columns, preferred_element_type=jnp.float32
    ).astype(jnp.bfloat16)
    per_group = orbitals // lax.axis_size("grp")
    regrouped = lax.all_to_all(
        lax.all_to_all(half_rows, "grp", split_axis=1, concat_axis=2, tiled=True),
        "aux",
        split_axis=1,
        concat_axis=0,
        tiled=True,
    )
    owned = per_group // lax.axis_size("aux")
    start_row = lax.axis_index("grp") * per_group + lax.axis_index("aux") * owned
    own_lists = lax.dynamic_slice_in_dim(block_lists, start_row, owned, 0)
    own_counts = lax.dynamic_slice_in_dim(block_counts, start_row, owned, 0)
    domain = jnp.sum(block_tables(own_lists, own_counts, block_total), axis=1)
    domain_mask = jnp.broadcast_to(domain[:, :, None], (owned, block_total, block_size)).reshape(
        owned, window
    )
    masked = regrouped * domain_mask[None]
    partial_value = jnp.einsum("pim,pin->mn", masked, masked, preferred_element_type=jnp.float32)
    return lax.psum_scatter(partial_value, ("grp", "aux"), scatter_dimension=0, tiled=True)


def solution(mesh):
    placed = (P("aux", "grp", None), P(), P(), P())
    return jax.shard_map(
        shards, mesh=mesh, in_specs=placed, out_specs=P(("grp", "aux"), None), check_vma=False
    )
```

profile of v0, /device:TPU:0, one launch (start us, length us, event | category | flops | bytes accessed | tf_op | source)
XLA Modules:
  0.0 363.8 jit_solution(13976031469346292998)
XLA Ops:
  6.5 1.1 copy.29
  7.6 0.8 copy.28
  8.4 0.7 iota_compare_fusion.1
  9.1 0.2 fusion
  9.4 0.2 copy.30
  9.5 13.9 %convert_bitcast_fusion = bf16[192,96,128]{2,1,0:T(8,128)(2,1)} fusion(bf16[512,96,1]{1,0,2:T(8,128)(2,1)S(1)} %bitcast.25, bf16[192,128,512]{2,1,0:T(8,128)(2,1)} %param.4), kind=kOutput, calls=%fused_computation.2 | convolution fusion | flops 2418278400 | bytes 29982720 | tf_op jit(solution)/shard_map/pmn,ni->pim/dot_general | solution.py:23
  23.5 4.2 %copy.32 = bf16[192,96,128]{2,0,1:T(8,128)(2,1)S(1)} copy(bf16[192,96,128]{2,1,0:T(8,128)(2,1)} %convert_bitcast_fusion) | data formatting | bytes 9437184 | tf_op jit(solution)/shard_map/convert_element_type | solution.py:25
  27.6 110.5 %all_to_all.36 = bf16[192,96,128]{2,0,1:T(8,128)(2,1)S(1)} all-to-all(bf16[192,96,128]{2,0,1:T(8,128)(2,1)S(1)} %copy.32), channel_id=1, replica_groups=mesh['grp'=4,'aux'=8] {'grp'}, dimensions={1} | all-to-all | bytes 9437184 | tf_op jit(solution)/shard_map/all_to_all | solution.py:28
  138.1 5.8 %copy.42 = bf16[192,4,24,128]{3,1,2,0:T(4,128)(2,1)} copy(bf16[192,4,24,128]{3,0,2,1:T(8,128)(2,1)S(1)} %bitcast.23) | data formatting | bytes 9437184 | tf_op jit(solution)/shard_map/all_to_all | solution.py:28
  143.9 8.0 %all_to_all.29 = bf16[192,24,512]{2,1,0:T(8,128)(2,1)} reshape(bf16[192,24,4,128]{3,2,1,0:T(4,128)(2,1)} %bitcast.24) | data formatting | bytes 9437184 | tf_op jit(solution)/shard_map/all_to_all | solution.py:28
  152.0 6.1 %copy.34 = bf16[192,24,512]{2,0,1:T(8,128)(2,1)} copy(bf16[192,24,512]{2,1,0:T(8,128)(2,1)} %all_to_all.29) | data formatting | bytes 9437184 | tf_op jit(solution)/shard_map/all_to_all | solution.py:28
  158.1 0.0 copy-start.1
  158.1 0.0 copy-start
  158.1 4.7 %all-to-all-start.1 = ((bf16[192,24,512]{2,0,1:T(8,128)(2,1)}), bf16[192,24,512]{2,0,1:T(8,128)(2,1)}, u32[]{:S(2)}, u32[]{:S(2)}) async-start(bf16[192,24,512]{2,0,1:T(8,128)(2,1)} %copy.34), calls=%async_computation.1 | async-start | bytes 9437184 | tf_op jit(solution)/shard_map/all_to_all | solution.py:27
  162.8 0.2 reduce-scatter.2.cloned.1.call-start
  163.0 0.0 copy-done.1
  163.1 0.1 dynamic_slice.7
  163.1 0.0 copy-done
  163.1 0.1 constant_dynamic-slice_fusion
  163.2 0.1 copy.36
  163.3 0.1 iota_compare_fusion.3
  163.4 0.1 fusion.7
  163.5 0.1 broadcast_in_dim.2
  163.5 0.1 mul.18
  163.6 53.9 %all-to-all-done.1 = bf16[192,24,512]{2,0,1:T(8,128)(2,1)} async-done(((bf16[192,24,512]{2,0,1:T(8,128)(2,1)}), bf16[192,24,512]{2,0,1:T(8,128)(2,1)}, u32[]{:S(2)}, u32[]{:S(2)}) %all-to-all-start.1) | async-done | bytes 4718624 | tf_op jit(solution)/shard_map/all_to_all | solution.py:27
  217.5 2.6 copy.35
  220.2 0.6 bitcast_multiply_fusion
  220.8 3.6 convolution_bitcast_fusion
  224.4 0.0 reduce-scatter.2.cloned.1.call-update
  224.4 132.5 %reduce-scatter.2.cloned.1.call-done = f32[16,512]{1,0:T(8,128)} async-done(((f32[512,512]{1,0:T(8,128)}), f32[16,512]{1,0:T(8,128)}) %reduce-scatter.2.cloned.1.call-update) | async-done | bytes 32784 | tf_op jit(solution)/shard_map/reduce_scatter | solution.py:44
Async XLA Ops:
  158.1 5.0 %copy-start.1 = (s32[96]{0:T(128)S(1)}, s32[96]{0:T(128)}, u32[]{:S(2)}) copy-start(s32[96]{0:T(128)} %param.7) | copy-start | bytes 1156
  158.1 5.1 %copy-start = (s32[96,8]{0,1:T(8,128)S(1)}, s32[96,8]{0,1:T(8,128)}, u32[]{:S(2)}) copy-start(s32[96,8]{0,1:T(8,128)} %param.6) | copy-start | bytes 9220
  158.1 59.5 %all-to-all-start.1 = ((bf16[192,24,512]{2,0,1:T(8,128)(2,1)}), bf16[192,24,512]{2,0,1:T(8,128)(2,1)}, u32[]{:S(2)}, u32[]{:S(2)}) async-start(bf16[192,24,512]{2,0,1:T(8,128)(2,1)} %copy.34), calls=%async_computation.1 | async-start | bytes 9437184 | tf_op jit(solution)/shard_map/all_to_all | solution.py:27
  162.8 194.1 %reduce-scatter.2.cloned.1.call-start = ((), (), s32[]{:S(2)}) async-start(), calls=%async_computation.3 | async-start | bytes 1081344 | tf_op jit(solution)/shard_map/reduce_scatter | solution.py:44
Sparse Core Ops, SparseCore 0:
  224.6 132.2 reduce-scatter.1
where the time goes:
time: 364 us
  waiting for transfers between devices  186 us (51%)
  blocking collectives  110 us (30%)
  local copies, waits for them, and re-layouts  29.2 us (8%)
  matrix products  17.8 us (5%)
  between operations  13.5 us (4%)
  starting transfers between devices  4.94 us (1%)
    reduce_scatter x1, waiting for transfers between devices, shards(): lax.psum_scatter(partial_value, ('grp', 'aux'), scatter_dimension=0, tile...  132 us
    all_to_all x1, blocking collectives, shards(): lax.all_to_all(half_rows, 'grp', split_axis=1, concat_axis=2, tiled=True)  110 us
    all_to_all x1, waiting for transfers between devices, shards(): lax.all_to_all(lax.all_to_all(half_rows, 'grp', split_axis=1, concat_axis...  53.9 us
    all_to_all x3, local copies, waits for them, and re-layouts, shards(): lax.all_to_all(half_rows, 'grp', split_axis=1, concat_axis=2, tiled=True)  19.9 us
    dot_general x1, matrix products, shards(): jnp.einsum('pmn,ni->pim', integrals, columns, preferred_element_type=jnp....  13.9 us
  transfers between devices with their start and end apart: 2, of which 2 were waited for; matrix products, arithmetic and copies ran while one was open for 0% of the time, Pallas kernels for 0%

commit v1 on v0

--- a/solution.py
+++ b/solution.py
@@ -23,21 +23,10 @@
     half_rows = jnp.einsum(
         "pmn,ni->pim", integrals, columns, preferred_element_type=jnp.float32
     ).astype(jnp.bfloat16)
-    per_group = orbitals // lax.axis_size("grp")
-    regrouped = lax.all_to_all(
-        lax.all_to_all(half_rows, "grp", split_axis=1, concat_axis=2, tiled=True),
-        "aux",
-        split_axis=1,
-        concat_axis=0,
-        tiled=True,
-    )
-    owned = per_group // lax.axis_size("aux")
-    start_row = lax.axis_index("grp") * per_group + lax.axis_index("aux") * owned
-    own_lists = lax.dynamic_slice_in_dim(block_lists, start_row, owned, 0)
-    own_counts = lax.dynamic_slice_in_dim(block_counts, start_row, owned, 0)
-    domain = jnp.sum(block_tables(own_lists, own_counts, block_total), axis=1)
-    domain_mask = jnp.broadcast_to(domain[:, :, None], (owned, block_total, block_size)).reshape(
-        owned, window
+    regrouped = lax.all_to_all(half_rows, "grp", split_axis=0, concat_axis=2, tiled=True)
+    domain = jnp.sum(selected, axis=1)
+    domain_mask = jnp.broadcast_to(domain[:, :, None], (orbitals, block_total, block_size)).reshape(
+        orbitals, window
     )
     masked = regrouped * domain_mask[None]
     partial_value = jnp.einsum("pim,pin->mn", masked, masked, preferred_element_type=jnp.float32)

time: 364 us -> 283 us (0.78)
  blocking collectives: 110 us -> 0 us
  waiting for transfers between devices: 186 us -> 238 us
  local copies, waits for them, and re-layouts: 29.2 us -> 2.23 us
  matrix products: 17.8 us -> 21.7 us
    all_to_all x1 -> x0, blocking collectives: 110 us -> none  [shards(): lax.all_to_all(half_rows, 'grp', split_axis=1, concat_axis=2, tiled=True)]
    all_to_all x1, waiting for transfers between devices: 53.9 us -> 104 us  [shards(): lax.all_to_all(half_rows, 'grp', split_axis=0, concat_axis=2, tiled=True)]
    all_to_all x4 -> x0, local copies, waits for them, and re-layouts: 22.6 us -> none  [the longest x3 19.9 us: shards(): lax.all_to_all(half_rows, 'grp', split_axis=1, concat_axis=2, tiled=True)]
    convert_element_type x1 -> x0, local copies, waits for them, and re-layouts: 4.16 us -> none  [shards(): half_rows = jnp.einsum('pmn,ni->pim', integrals, columns, preferred_eleme...]
    dot_general x1, matrix products: 3.6 us -> 7.42 us  [shards(): jnp.einsum('pim,pin->mn', masked, masked, preferred_element_type=jnp.floa...]
where the time goes in v1:
time: 283 us
  waiting for transfers between devices  238 us (84%)
  matrix products  21.7 us (8%)
  between operations  13.4 us (5%)
  starting transfers between devices  6.32 us (2%)
    reduce_scatter x1, waiting for transfers between devices, shards(): lax.psum_scatter(partial_value, ('grp', 'aux'), scatter_dimension=0, tile...  134 us
    all_to_all x1, waiting for transfers between devices, shards(): lax.all_to_all(half_rows, 'grp', split_axis=0, concat_axis=2, tiled=True)  104 us
    dot_general x1, matrix products, shards(): jnp.einsum('pmn,ni->pim', integrals, columns, preferred_element_type=jnp....  14 us
    dot_general x1, matrix products, shards(): jnp.einsum('pim,pin->mn', masked, masked, preferred_element_type=jnp.floa...  7.42 us
    all_to_all x1, starting transfers between devices, shards(): lax.all_to_all(half_rows, 'grp', split_axis=0, concat_axis=2, tiled=True)  6.32 us
  transfers between devices with their start and end apart: 2, of which 2 were waited for; matrix products, arithmetic and copies ran while one was open for 0% of the time, Pallas kernels for 0%

profile of v1, /device:TPU:0, one launch (start us, length us, event | category | flops | bytes accessed | tf_op | source)
XLA Modules:
  0.0 283.0 jit_solution(3984684885188107594)
XLA Ops:
  6.5 0.8 copy.14
  7.3 0.7 iota_compare_fusion.1
  8.1 1.1 copy.15
  9.1 0.2 fusion.4
  9.4 0.2 copy.16
  9.5 14.0 %convert_bitcast_fusion = bf16[192,96,128]{2,1,0:T(8,128)(2,1)} fusion(bf16[512,96,1]{1,0,2:T(8,128)(2,1)S(1)} %bitcast.22, bf16[192,128,512]{2,1,0:T(8,128)(2,1)} %param.4), kind=kOutput, calls=%fused_computation.3 | convolution fusion | flops 2418278400 | bytes 29982720 | tf_op jit(solution)/shard_map/pmn,ni->pim/dot_general | solution.py:23
  23.5 6.3 %all-to-all-start = ((bf16[192,96,128]{2,1,0:T(8,128)(2,1)}), bf16[192,96,128]{2,1,0:T(8,128)(2,1)}, u32[]{:S(2)}, u32[]{:S(2)}) async-start(bf16[192,96,128]{2,1,0:T(8,128)(2,1)} %convert_bitcast_fusion), calls=%async_computation | async-start | bytes 9437184 | tf_op jit(solution)/shard_map/all_to_all | solution.py:26
  29.9 0.0 reduce-scatter.2.cloned.1.call-start
  29.9 0.2 fusion.8
  30.1 0.1 copy.19
  30.2 0.1 copy.20
  30.3 104.3 %all-to-all-done = bf16[192,96,128]{2,1,0:T(8,128)(2,1)} async-done(((bf16[192,96,128]{2,1,0:T(8,128)(2,1)}), bf16[192,96,128]{2,1,0:T(8,128)(2,1)}, u32[]{:S(2)}, u32[]{:S(2)}) %all-to-all-start) | async-done | bytes 4718624 | tf_op jit(solution)/shard_map/all_to_all | solution.py:26
  134.6 7.4 %fusion.3 = f32[512,512]{1,0:T(8,128)} fusion(bf16[4,48,12,8,128]{4,3,2,1,0:T(8,128)(2,1)} %bitcast.10, bf16[96,512]{1,0:T(8,128)(2,1)S(1)} %copy.20), kind=kOutput, calls=%fused_computation.5 | convolution fusion | flops 2418278400 | bytes 5865472 | tf_op jit(solution)/shard_map/pim,pin->mn/dot_general | solution.py:32
  142.0 0.0 reduce-scatter.2.cloned.1.call-update
  142.1 134.1 %reduce-scatter.2.cloned.1.call-done = f32[16,512]{1,0:T(8,128)} async-done(((f32[512,512]{1,0:T(8,128)}), f32[16,512]{1,0:T(8,128)}) %reduce-scatter.2.cloned.1.call-update) | async-done | bytes 32784 | tf_op jit(solution)/shard_map/reduce_scatter | solution.py:33
  (1 shorter events, 0.0 us)
Async XLA Ops:
  23.5 111.1 %all-to-all-start = ((bf16[192,96,128]{2,1,0:T(8,128)(2,1)}), bf16[192,96,128]{2,1,0:T(8,128)(2,1)}, u32[]{:S(2)}, u32[]{:S(2)}) async-start(bf16[192,96,128]{2,1,0:T(8,128)(2,1)} %convert_bitcast_fusion), calls=%async_computation | async-start | bytes 9437184 | tf_op jit(solution)/shard_map/all_to_all | solution.py:26
  29.9 246.3 %reduce-scatter.2.cloned.1.call-start = ((), (), s32[]{:S(2)}) async-start(), calls=%async_computation.2 | async-start | bytes 1081344 | tf_op jit(solution)/shard_map/reduce_scatter | solution.py:33
Sparse Core Ops, SparseCore 0:
  142.2 133.8 reduce-scatter.1

commit v2 on v1

--- a/solution.py
+++ b/solution.py
@@ -1,7 +1,15 @@
+import functools
+
 import jax
 import jax.numpy as jnp
 from jax import lax
+from jax.experimental import pallas as pl
+from jax.experimental.pallas import tpu as pltpu
 from jax.sharding import PartitionSpec as P
+
+LANES = 128
+MESH = pl.DeviceIdType.MESH
+LEVELS = (64, 80)
 
 
 def block_tables(block_rows, counts, block_total):
@@ -10,6 +18,238 @@
     target = lax.broadcasted_iota(jnp.int32, block_rows.shape + (block_total,), 2)
     onehot = (block_rows[:, :, None] == target) & live_slot[:, :, None]
     return onehot.astype(jnp.bfloat16)
+
+
+def fused_kernel(
+    groups, planes, parts, step, slots,
+    integrals, packed_columns, spread, out,
+    loaded, outgoing, arrived, unpacked, total, ordered,
+    core_in, core_sum, plane_in, plane_sum, group_in,
+    load_sem, half_send, half_recv, core_send, core_recv,
+    plane_send, plane_recv, group_send, group_recv,
+):
+    grp, aux = lax.axis_index("grp"), lax.axis_index("aux")
+    core, place = aux % 2, aux // 2
+    other_core = place * 2 + (1 - core)
+    orbitals = spread.shape[1] // 2
+    rows_out = out.shape[0]
+    depth = step * parts
+
+    def group_at(shift):
+        return (grp + shift) % groups
+
+    def place_at(shift):
+        return (place + shift) % planes
+
+    order = [(shift + 1) % groups for shift in range(groups)]
+
+    def load(part, shift):
+        first = group_at(shift) * depth + part * step
+        return pltpu.make_async_copy(
+            integrals.at[pl.ds(first, step)], loaded.at[shift], load_sem.at[shift]
+        )
+
+    for shift in order:
+        load(0, shift).start()
+
+    barrier = pltpu.get_barrier_semaphore()
+    partners = [(group_at(shift), aux) for shift in range(1, groups)]
+    partners += [(grp, place_at(shift) * 2 + core) for shift in range(1, planes)]
+    partners += [(grp, other_core)]
+    for partner in partners:
+        pl.semaphore_signal(barrier, inc=1, device_id=partner, device_id_type=MESH)
+    pl.semaphore_wait(barrier, len(partners))
+
+    def half_copy(part, shift, landing):
+        return pltpu.make_async_remote_copy(
+            src_ref=outgoing.at[shift - 1, part],
+            dst_ref=arrived.at[landing, part],
+            send_sem=half_send.at[shift - 1, part],
+            recv_sem=half_recv.at[shift - 1, part],
+            device_id=(group_at(shift), aux),
+            device_id_type=MESH,
+        )
+
+    def lower_block(shape):
+        return lax.broadcasted_iota(jnp.int32, shape, 1) % LANES < LANES // 2
+
+    def transform(part, carry):
+        for shift in order:
+            load(part, shift).wait()
+            for pair in range(step // 2):
+                rows = loaded[shift, 2 * pair : 2 * pair + 2].reshape(2 * LANES, loaded.shape[3])
+                both = lax.dot_general(
+                    packed_columns[...], rows, (((1,), (1,)), ((), ())),
+                    preferred_element_type=jnp.float32,
+                )
+                half = jnp.where(
+                    lower_block((slots, 2 * LANES)), both[:slots], both[slots:]
+                ).astype(jnp.bfloat16)
+                columns = slice(pair * 2 * LANES, (pair + 1) * 2 * LANES)
+                if shift:
+                    outgoing[shift - 1, part, :, columns] = half
+                else:
+                    arrived[grp, part, :, columns] = half
+
+            @pl.when(part + 1 < parts)
+            def _():
+                load(part + 1, shift).start()
+
+            if shift:
+                half_copy(part, shift, grp).start()
+        return carry
+
+    lax.fori_loop(0, parts, transform, 0)
+    total[...] = jnp.zeros_like(total)
+
+    def contract(part, carry):
+        for shift in range(1, groups):
+            half_copy(part, shift, group_at(groups - shift)).wait_recv()
+        for source in range(groups):
+            for pair in range(step // 2):
+                columns = slice(pair * 2 * LANES, (pair + 1) * 2 * LANES)
+                both = jnp.dot(
+                    spread[source], arrived[source, part, :, columns],
+                    preferred_element_type=jnp.float32,
+                )
+                half = jnp.where(
+                    lower_block((orbitals, 2 * LANES)), both[:orbitals], both[orbitals:]
+                ).astype(jnp.bfloat16)
+                for side in range(2):
+                    first = (2 * pair + side) * orbitals
+                    unpacked[first : first + orbitals, source * LANES : (source + 1) * LANES] = (
+                        half[:, side * LANES : (side + 1) * LANES]
+                    )
+        total[...] += lax.dot_general(
+            unpacked[...], unpacked[...], (((0,), (0,)), ((), ())),
+            preferred_element_type=jnp.float32,
+        )
+        return carry
+
+    lax.fori_loop(0, parts, contract, 0)
+
+    for group in range(groups):
+        for spot in range(planes):
+            for side in range(2):
+                first = ((group * planes + spot) * 2 + side) * rows_out
+                ordered[side, spot, group] = total[first : first + rows_out, :]
+
+    def core_copy(shift):
+        return pltpu.make_async_remote_copy(
+            src_ref=ordered.at[1 - core, place_at(shift)],
+            dst_ref=core_in.at[shift],
+            send_sem=core_send.at[shift],
+            recv_sem=core_recv.at[shift],
+            device_id=(grp, other_core),
+            device_id_type=MESH,
+        )
+
+    def plane_copy(shift):
+        return pltpu.make_async_remote_copy(
+            src_ref=core_sum.at[shift],
+            dst_ref=plane_in.at[shift - 1],
+            send_sem=plane_send.at[shift - 1],
+            recv_sem=plane_recv.at[shift - 1],
+            device_id=(grp, place_at(shift) * 2 + core),
+            device_id_type=MESH,
+        )
+
+    def group_copy(shift):
+        return pltpu.make_async_remote_copy(
+            src_ref=plane_sum.at[group_at(shift)],
+            dst_ref=group_in.at[shift - 1],
+            send_sem=group_send.at[shift - 1],
+            recv_sem=group_recv.at[shift - 1],
+            device_id=(group_at(shift), aux),
+            device_id_type=MESH,
+        )
+
+    places = [(shift + 1) % planes for shift in range(planes)]
+    for shift in places:
+        core_copy(shift).start()
+    for shift in places:
+        core_copy(shift).wait_recv()
+        core_sum[shift] = ordered[core, place_at(shift)] + core_in[shift]
+        if shift:
+            plane_copy(shift).start()
+    for shift in range(1, planes):
+        plane_copy(shift).wait_recv()
+    summed = core_sum[0]
+    for shift in range(1, planes):
+        summed += plane_in[shift - 1]
+    plane_sum[...] = summed
+    for shift in range(1, groups):
+        group_copy(shift).start()
+    for shift in range(1, groups):
+        group_copy(shift).wait_recv()
+    result = plane_sum[grp]
+    for shift in range(1, groups):
+        result += group_in[shift - 1]
+    out[...] = result
+
+    def drain(part, carry):
+        for shift in range(1, groups):
+            half_copy(part, shift, grp).wait_send()
+        return carry
+
+    lax.fori_loop(0, parts, drain, 0)
+    for shift in range(planes):
+        core_copy(shift).wait_send()
+    for shift in range(1, planes):
+        plane_copy(shift).wait_send()
+    for shift in range(1, groups):
+        group_copy(shift).wait_send()
+
+
+def fused(slots, ident, groups, planes, parts, integrals, columns, live, rank):
+    aux_rows, group_rows, window = integrals.shape
+    blocks, orbitals = live.shape
+    step = aux_rows // groups // parts
+    rows_out = window // (groups * planes * 2)
+    slot = lax.broadcasted_iota(jnp.int32, (blocks, orbitals, slots), 2)
+    spread = ((rank[:, :, None] == slot) & live[:, :, None]).astype(jnp.bfloat16)
+    own = lax.dynamic_slice_in_dim(spread, lax.axis_index("grp") * 2, 2, 0)
+    packed_columns = jnp.einsum(
+        "bis,ni->bsn", own, columns, preferred_element_type=jnp.float32
+    ).astype(jnp.bfloat16).reshape(2 * slots, window)
+    spread = spread.reshape(groups, 2 * orbitals, slots)
+    bf16, f32, dma = jnp.bfloat16, jnp.float32, pltpu.SemaphoreType.DMA
+    piece = (groups, rows_out, window)
+    return pl.pallas_call(
+        functools.partial(fused_kernel, groups, planes, parts, step, slots),
+        out_shape=jax.ShapeDtypeStruct((rows_out, window), f32),
+        in_specs=[
+            pl.BlockSpec(memory_space=pl.ANY),
+            pl.BlockSpec(memory_space=pltpu.VMEM),
+            pl.BlockSpec(memory_space=pltpu.VMEM),
+        ],
+        out_specs=pl.BlockSpec(memory_space=pltpu.VMEM),
+        scratch_shapes=[
+            pltpu.VMEM((groups, step, group_rows, window), bf16),
+            pltpu.VMEM((groups - 1, parts, slots, step * LANES), bf16),
+            pltpu.VMEM((groups, parts, slots, step * LANES), bf16),
+            pltpu.VMEM((step * orbitals, window), bf16),
+            pltpu.VMEM((window, window), f32),
+            pltpu.VMEM((2, planes) + piece, f32),
+            pltpu.VMEM((planes,) + piece, f32),
+            pltpu.VMEM((planes,) + piece, f32),
+            pltpu.VMEM((planes - 1,) + piece, f32),
+            pltpu.VMEM(piece, f32),
+            pltpu.VMEM((groups - 1, rows_out, window), f32),
+            dma((groups,)),
+            dma((groups - 1, parts)),
+            dma((groups - 1, parts)),
+            dma((planes,)),
+            dma((planes,)),
+            dma((planes - 1,)),
+            dma((planes - 1,)),
+            dma((groups - 1,)),
+            dma((groups - 1,)),
+        ],
+        compiler_params=pltpu.CompilerParams(
+            collective_id=ident, has_side_effects=True, vmem_limit_bytes=48 * 1024 * 1024
+        ),
+    )(integrals, packed_columns, spread)
 
 
 def shards(integrals, coefficients, block_lists, block_counts):
@@ -20,11 +260,30 @@
     selected = block_tables(block_lists, block_counts, block_total)
     columns = jnp.einsum("ikb,ikj->bji", selected, coefficients, preferred_element_type=jnp.float32)
     columns = columns.astype(jnp.bfloat16).reshape(window, orbitals)
+    domain = jnp.sum(selected, axis=1)
+    groups, planes = lax.axis_size("grp"), lax.axis_size("aux") // 2
+    per_group = integrals.shape[0] // groups
+    parts = 4
+    if (
+        2 * block_size == LANES == integrals.shape[1]
+        and per_group % (2 * parts) == 0
+        and orbitals % 16 == 0
+        and orbitals <= 128
+    ):
+        live = domain.T > 0
+        rank = jnp.cumsum(live.astype(jnp.int32), axis=1) - 1
+        fullest = jnp.max(rank[:, -1]) + 1
+        levels = [level for level in LEVELS if level < orbitals] + [orbitals]
+        branches = [
+            functools.partial(fused, level, ident, groups, planes, parts)
+            for ident, level in enumerate(levels)
+        ]
+        choice = sum((fullest > level).astype(jnp.int32) for level in levels[:-1])
+        return lax.switch(choice, branches, integrals, columns, live, rank)
     half_rows = jnp.einsum(
         "pmn,ni->pim", integrals, columns, preferred_element_type=jnp.float32
     ).astype(jnp.bfloat16)
     regrouped = lax.all_to_all(half_rows, "grp", split_axis=0, concat_axis=2, tiled=True)
-    domain = jnp.sum(selected, axis=1)
     domain_mask = jnp.broadcast_to(domain[:, :, None], (orbitals, block_total, block_size)).reshape(
         orbitals, window
     )

time: 283 us -> 95.5 us (0.34)
  waiting for transfers between devices: 238 us -> 0 us
  Pallas kernels: 0 us -> 89.1 us
  matrix products: 21.7 us -> 0.44 us
  between operations: 13.4 us -> 0.69 us
  starting transfers between devices: 6.32 us -> 0 us
    reduce_scatter x1 -> x0, waiting for transfers between devices: 134 us -> none  [shards(): lax.psum_scatter(partial_value, ('grp', 'aux'), scatter_dimension=0, tile...]
    all_to_all x1 -> x0, waiting for transfers between devices: 104 us -> none  [shards(): lax.all_to_all(half_rows, 'grp', split_axis=0, concat_axis=2, tiled=True)]
    pallas_call x0 -> x1, Pallas kernels: none -> 89.1 us  [fused(): pl.pallas_call(functools.partial(fused_kernel, groups, planes, parts, ste...]
    dot_general x2 -> x1, matrix products: 21.4 us -> 0.19 us  [fused(): jnp.einsum('bis,ni->bsn', own, columns, preferred_element_type=jnp.float32)]
    all_to_all x1 -> x0, starting transfers between devices: 6.32 us -> none  [shards(): lax.all_to_all(half_rows, 'grp', split_axis=0, concat_axis=2, tiled=True)]
  transfers between devices with their start and end apart: 2 -> 0, of which waited for: 2 -> 0; matrix products, arithmetic and copies ran while one was open for 0% -> 0% of each run, Pallas kernels for 0% -> 0%
where the time goes in v2:
time: 95.5 us; the launch traced here: 95.4 us
  Pallas kernels  89.1 us (93%)
  local copies, waits for them, and re-layouts  2.88 us (3%)
  other arithmetic  2.19 us (2%)
    pallas_call x1, Pallas kernels, fused(): pl.pallas_call(functools.partial(fused_kernel, groups, planes, parts, ste...  89.1 us
    unnamed x3, local copies, waits for them, and re-layouts  2.46 us

profile of v2, /device:TPU:0, one launch (start us, length us, event | category | flops | bytes accessed | tf_op | source)
XLA Modules:
  0.0 95.4 jit_solution(10789337571172229325)
XLA Ops:
  0.0 0.7 iota_compare_fusion.7
  0.7 0.8 copy.36
  1.5 0.2 fusion.22
  1.7 0.1 copy.37
  1.8 0.3 reduce_window_sum.11
  2.1 0.7 slice_reduce_fusion
  3.4 1.1 %copy.38 = bf16[96,8,64]{2,1,0:T(8,128)(2,1)S(1)} copy(bf16[96,8,64]{0,2,1:T(8,128)(2,1)} %param.8) | data formatting | bytes 196608 | tf_op args[1]
  4.5 0.2 fusion.18
  4.8 90.0 %conditional.1 = (f32[16,512]{1,0:T(8,128)S(1)}) conditional(s32[]{:T(128)} %clamp.3, (s32[8,96]{1,0:T(8,128)S(1)}, pred[8,96]{1,0:T(8,128)(4,1)S(1)}, bf16[8,64,96]{1,0,2:T(8,128)(2,1)S(1)}, bf16[192,128,512]{2,1,0:T(8,128)(2,1)}) %tuple.14, (s32[8,96]{1,0:T(8,128)S(1)}, pred[8,96]{1,0:T(8,128)(4,1)S(1)}, ...), branch_computations={%region_3.4_spmd, %region_4.5_spmd, %region_5.6_spmd} | conditional | flops 19230728 | bytes 653470 | solution.py:282
  4.8 0.1 and.41
  4.9 0.1 eq.38
  5.0 0.2 copy.39
  5.1 0.2 convolution_convert_fusion
  5.3 0.3 fusion.1.spread
  5.6 89.1 %branch_0_fun.1 = f32[16,512]{1,0:T(8,128)S(1)} custom-call(bf16[192,128,512]{2,1,0:T(8,128)(2,1)} %get-tuple-element.52.integrals, bf16[128,512]{1,0:T(8,128)(2,1)S(1)} %bitcast.23, bf16[4,192,64]{2,1,0:T(8,128)(2,1)S(1)} %fusion.1.spread), custom_call_target="tpu_custom_call" | custom-call | tf_op jit(solution)/shard_map/cond/branch_0_fun/pallas_call | solution.py:218
  94.7 0.6 copy.52
  (4 shorter events, 0.0 us)
